TPU v7x, 256 devices: a whole 4x4x8 slice. The times are simulated.
256 devices in a mesh: xp: 8 (over z), zp: 8 (over y_lo, x), gy: 4 (over y_hi, core).
Axes of the slice: x: 4, y: 4 (y_hi: 2, y_lo: 2; y = y_hi * 2 + y_lo), z: 8, core: 2. Of those that a mesh axis runs over, the one named last changes fastest.
Arguments:
- fields: float32 [4, 12, 4096, 4096], P(None, 'gy', ('xp', 'zp')), may hold values from -12 to 12
Outputs:
- filtered: float32 [10, 12, 512, 512], P(None, 'gy', ('xp', 'zp'))
All inputs are finite; a program needn't handle non-finite values.
Results may differ from a plain program's by a relative error of at most 0.00012.
Values sent between devices are 32-bit elements; how exact they have to be, the bound alone decides.
A program may use at most 192 MiB of HBM per device.

v0:
```python
import functools

import jax
import jax.numpy as jnp
import numpy as np
from jax import lax
from jax.experimental import pallas as pl
from jax.experimental.pallas import tpu as pltpu
from jax.sharding import PartitionSpec as P

MESH = pl.DeviceIdType.MESH
F32, BF16 = jnp.float32, jnp.bfloat16
PAIRS = ((0, 0), (1, 1), (0, 1), (0, 2), (1, 3))
PRODUCTS = (0, 1, 4, 5, 8, 2, 3, 9, 6, 7)
PLANES, ROWS, NX = 3, 64, 4096
BLOCKS = 4
PIECES = 2 * PLANES
SEND_AT, MID_AT = 1, 3


def gauss():
    t = np.arange(-16, 17).astype(np.float64)
    e = np.exp(-6.0 * t * t / 256.0)
    return e / e.sum()


G = [float(v) for v in gauss()[16:]]


def x_weights():
    g = gauss()
    w = np.zeros((1280, 128), np.float64)

    def put(row, x, col, coarse):
        t = x - 8 * coarse
        if abs(t) <= 16:
            w[row, col] = g[t + 16]

    for x in range(1024):
        for c in range(128):
            put(x, x, c, c)
    for x in range(128):
        put(1024 + x, x, 126, -2)
        put(1024 + x, x, 127, -1)
        put(1152 + x, 896 + x, 0, 128)
        put(1152 + x, 896 + x, 1, 129)
    w = w.astype(np.float32)
    high = w.astype(jnp.bfloat16)
    low = (w - high.astype(np.float32)).astype(jnp.bfloat16)
    return np.concatenate([high, low], axis=1)


def z_stage(load, row):
    acc = {}

    def add(key, value):
        acc[key] = value if key not in acc else acc[key] + value

    for b in (1, 2, 3):
        near = [load(f, b) for f in range(4)]
        far = [load(f, 8 - b) for f in range(4)]
        for p, (i, j) in enumerate(PAIRS):
            x, y = near[i] * near[j], far[i] * far[j]
            plus, minus = x + y, x - y
            add((p, 0), plus * ((G[b] + G[8 - b]) / 2))
            add((p, 1), minus * ((G[b] - G[8 - b]) / 2))
            add((p, 2), plus * ((G[8 + b] + G[16 - b]) / 2))
            add((p, 3), minus * ((G[8 + b] - G[16 - b]) / 2))
    four = [load(f, 4) for f in range(4)]
    zero = [load(f, 0) for f in range(4)]
    low_half = row < 4
    ends = (row == 0) | (row == 7)
    four_ends = (row < 2) | (row > 5)
    out = []
    for p, (i, j) in enumerate(PAIRS):
        r4, r0 = four[i] * four[j], zero[i] * zero[j]
        r8, r16 = r0 * G[8], r0 * G[16]
        d0, d1 = acc[p, 0] + r4 * G[4], acc[p, 2] + r4 * G[12]
        e0, e1 = acc[p, 1], acc[p, 3]
        s0, down1 = (d0 + e0) + r0 * G[0], (d0 - e0) + r8
        up1, down2 = (d1 + e1) + r8, (d1 - e1) + r16
        u1, u2 = pltpu.roll(up1, 7, 0), pltpu.roll(r16, 6, 0)
        v1, v2 = pltpu.roll(down1, 1, 0), pltpu.roll(down2, 2, 0)
        t1, t2 = jnp.where(low_half, v1, u1), jnp.where(low_half, v2, u2)
        w1, w2 = jnp.where(ends, t1, 0.0), jnp.where(four_ends, t2, 0.0)
        out.append((s0 + ((u1 + v1) - w1) + ((u2 + v2) - w2), t2 + w1))
    return out


def turn(x, shift):
    shift %= 128
    return pltpu.roll(x, shift, 1) if shift else x


def kernel(
    sizes, f_hbm, w_hbm, o_ref, fields, w_ref, held, main_x, leak_x, sent1, got1, sent2, got2, whole, beside,
    f_sem, w_sem, s1_sem, r1_sem, s2_sem, r2_sem, sy_sem, ry_sem,
):
    n_xp, n_zp, n_gy = sizes
    xp, zp, gy = lax.axis_index("xp"), lax.axis_index("zp"), lax.axis_index("gy")
    has_prev, has_next = gy > 0, gy < n_gy - 1

    def tile_copy(unit, h):
        tile = lax.rem(unit, BLOCKS) * 8 + h
        lanes = pl.ds(pl.multiple_of(tile * 128, 128), 128)
        plane = lax.rem(2 * (unit // BLOCKS), 3)
        return pltpu.make_async_copy(
            f_hbm.at[:, plane, :, lanes], fields.at[unit, h], f_sem.at[unit, h]
        )

    def fetch(unit):
        def one(h, carry):
            tile_copy(unit, h).start()
            return carry

        lax.fori_loop(0, 8, one, 0)

    weights = pltpu.make_async_copy(w_hbm, w_ref, w_sem)
    weights.start()
    fetch(0)
    for unit in range(1, BLOCKS):
        fetch(unit)

    barrier = pltpu.get_barrier_semaphore()

    def greet(**where):
        pl.semaphore_signal(barrier, inc=1, device_id=where, device_id_type=MESH)

    for k in range(1, n_zp):
        greet(zp=lax.rem(zp + k, n_zp))
    for k in range(1, n_xp):
        greet(xp=lax.rem(xp + k, n_xp))

    @pl.when(has_prev)
    def _():
        greet(gy=gy - 1)

    @pl.when(has_next)
    def _():
        greet(gy=gy + 1)

    def meet():
        beside_it = has_prev.astype(jnp.int32) + has_next.astype(jnp.int32)
        pl.semaphore_wait(barrier, n_xp + n_zp - 2 + beside_it)

    @pl.when(jnp.logical_not(has_prev))
    def _():
        beside[0] = jnp.zeros(beside.shape[1:], F32)

    @pl.when(jnp.logical_not(has_next))
    def _():
        beside[1] = jnp.zeros(beside.shape[1:], F32)

    row = lax.broadcasted_iota(jnp.int32, (8, 128), 0)
    lane = lax.broadcasted_iota(jnp.int32, (8, 128), 1)
    lane64 = lax.broadcasted_iota(jnp.int32, (64, 128), 1)
    main_x[...] = jnp.zeros(main_x.shape, F32)
    leak_x[...] = jnp.zeros(leak_x.shape, F32)
    got1[PIECES] = jnp.zeros(got1.shape[1:], F32)

    def filter_z(piece, block, h):
        slot = block % 2
        unit = (piece // 2) * BLOCKS + block
        half = lax.rem(piece, 2)
        names = (2 * half, 1 + 2 * half, 2 - half, 3 - 3 * half)

        def load(f, b):
            return fields[unit, h, names[f], pl.ds(b, 8, stride=8), :]

        rows = z_stage(load, row)
        four_ends = (row < 2) | (row > 5)
        groups = [main for main, _ in rows]
        for a in (0, 2):
            groups.append(jnp.where(four_ends, rows[a][1], pltpu.roll(rows[a + 1][1], 4, 0)))
        groups.append(jnp.where(four_ends, rows[4][1], 0.0))
        for k in range(4):
            both = jnp.concatenate(groups[2 * k : 2 * k + 2], axis=0)
            high = both.astype(BF16)
            held[slot, h, 0, k] = high
            held[slot, h, 1, k] = (both - high.astype(F32)).astype(BF16)

    def filter_x(piece, block):
        cells = [held[block % 2, h].reshape(128, 128) for h in range(8)]

        def product(values, weight):
            r = jnp.dot(values, weight, preferred_element_type=F32)
            return r[:64, :128] + r[64:, :128] + r[:64, 128:]

        main_x[block] = product(jnp.concatenate(cells, axis=1), w_ref[0:1024])
        leak_x[block] = product(jnp.concatenate([cells[0], cells[7]], axis=1), w_ref[1024:1280])

    def transpose(piece, block):
        before, after = leak_x[(block + 3) % BLOCKS], leak_x[(block + 1) % BLOCKS]
        x = main_x[block] + jnp.where(lane64 < 2, before, jnp.where(lane64 > 125, after, 0.0))
        y = jnp.transpose(jnp.concatenate([x, pltpu.roll(x, 64, 1)], axis=0))
        sent1[piece, :, block] = y[:64].reshape(8, 8, 128)

    def copy1(piece, to):
        return pltpu.make_async_remote_copy(
            src_ref=sent1.at[piece, to],
            dst_ref=got1.at[piece, zp],
            send_sem=s1_sem.at[piece],
            recv_sem=r1_sem.at[piece],
            device_id={"zp": to},
            device_id_type=MESH,
        )

    def copy2(piece, to):
        return pltpu.make_async_remote_copy(
            src_ref=sent2.at[piece, to],
            dst_ref=got2.at[piece, xp],
            send_sem=s2_sem.at[piece],
            recv_sem=r2_sem.at[piece],
            device_id={"xp": to},
            device_id_type=MESH,
        )

    def all1(piece):
        return pltpu.make_async_remote_copy(
            src_ref=sent1.at[piece, pl.ds(0, n_zp - 1)],
            dst_ref=got1.at[piece, pl.ds(0, n_zp - 1)],
            send_sem=s1_sem.at[piece],
            recv_sem=r1_sem.at[piece],
            device_id={"zp": lax.rem(zp + 1, n_zp)},
            device_id_type=MESH,
        )

    def all2(piece):
        return pltpu.make_async_remote_copy(
            src_ref=sent2.at[piece, pl.ds(0, n_xp - 1)],
            dst_ref=got2.at[piece, pl.ds(0, n_xp - 1)],
            send_sem=s2_sem.at[piece],
            recv_sem=r2_sem.at[piece],
            device_id={"xp": lax.rem(xp + 1, n_xp)},
            device_id_type=MESH,
        )

    def y_copy(side):
        return pltpu.make_async_remote_copy(
            src_ref=whole.at[1 - side],
            dst_ref=beside.at[side],
            send_sem=sy_sem.at[side],
            recv_sem=ry_sem.at[side],
            device_id={"gy": gy + 1 - 2 * side},
            device_id_type=MESH,
        )

    def start(side):
        @pl.when(has_next if side == 0 else has_prev)
        def _():
            y_copy(side).start()

    def send1(piece):
        for k in range(1, n_zp):
            copy1(piece, lax.rem(zp + k, n_zp)).start()
        got1[piece, zp] = sent1[piece, zp]

    def send2(piece):
        for k in range(1, n_xp):
            copy2(piece, lax.rem(xp + k, n_xp)).start()
        got2[piece, xp] = sent2[piece, xp]

    group, within = lane // 8, lax.rem(lane, 8)
    outer = (lane < 2) | (lane > 125) | ((lane > 61) & (lane < 66))
    left = lane < 64
    first_two = lax.rem(lane, 4) < 2

    def middle(piece, block):
        v = [got1[piece, k, block] for k in range(8)]
        for s in (4, 2, 1):
            bit = (group & s) == 0
            for a in range(8):
                if a & s == 0:
                    x, y = v[a], v[a + s]
                    v[a] = jnp.where(bit, x, turn(y, 8 * s))
                    v[a + s] = jnp.where(bit, turn(x, -8 * s), y)
            yield
        out = None
        for j in range(5):
            e, shift = v[5 + j // 2], 8 if j % 2 == 0 else 4
            z = jnp.where(within < 2, turn(e, shift), jnp.where(within > 5, turn(e, -shift), 0.0))
            v[j] = v[j] + jnp.where(outer, 0.0, z)
            z = turn(jnp.where(outer, z, 0.0), 4 * j + 2)
            out = z if out is None else out + z
        yield
        w = [turn(x, 64) for x in v[:5]]
        flip = turn(out, 64)
        rest = (jnp.where(first_two, flip, out), jnp.where(first_two, out, flip))
        for k in range(2):
            low = v if k == 0 else w
            high = w if k == 0 else v
            to = 2 * block + k
            sent2[piece, to, 0] = jnp.where(left, low[0], high[1])
            sent2[piece, to, 1] = jnp.where(left, low[2], high[3])
            sent2[piece, to, 2] = jnp.where(left, low[4], rest[k])

    def last(piece):
        all2(piece).wait_recv()
        plane, half = piece // 2, lax.rem(piece, 2)
        e = [got2[piece, d, 2] for d in range(8)]
        for j in range(5):
            m = [got2[piece, d, j // 2] for d in range(8)]
            near = [turn(x, -2 - 4 * j) for x in e]
            far = [turn(x, 62 - 4 * j) for x in e]
            for g in range(4):
                a, b = m[2 * g], m[2 * g + 1]
                if j % 2 == 0:
                    main = jnp.where(left, a, turn(b, 64))
                else:
                    main = jnp.where(left, turn(a, 64), b)
                z = jnp.where(lane < 2, far[(2 * g + 7) % 8], far[(2 * g + 2) % 8])
                z = jnp.where((lane > 61) & (lane < 64), near[2 * g + 1], z)
                z = jnp.where((lane > 63) & (lane < 66), near[2 * g], z)
                whole[plane, half * 5 + j, :, pl.ds(g * 128, 128)] = main + jnp.where(outer, z, 0.0)

    def run(*parts):
        parts = list(parts)
        while parts:
            parts = [part for part in parts if next(part, parts) is not parts]

    def one_piece(piece, carry):
        before = jnp.where(piece >= SEND_AT, piece - SEND_AT, PIECES)
        early = jnp.where(piece >= MID_AT, piece - MID_AT, PIECES)
        for block in range(BLOCKS):

            @pl.when(lax.rem(piece, 2) == 0)
            def _():
                for h in range(8):
                    tile_copy((piece // 2) * BLOCKS + block, h).wait()

            if block == 0:

                @pl.when(piece == 0)
                def _():
                    weights.wait()

                @pl.when(lax.rem(piece, 2) == 0)
                def _():
                    @pl.when(piece // 2 < PLANES - 1)
                    def _():
                        for later in range(BLOCKS):
                            fetch((piece // 2 + 1) * BLOCKS + later)

            if block == 2:

                @pl.when(piece >= MID_AT)
                def _():
                    all1(early).wait_recv()

            work = []
            if block == 1:
                for part in range(BLOCKS):
                    transpose(before, part)
            if block == 2:
                work = [middle(early, part) for part in range(BLOCKS)]
            filter_x(piece, (block + 3) % BLOCKS)
            for h in range(8):
                work = [part for part in work if next(part, work) is not work]
                filter_z(piece, block, h)
            run(*work)
            if block == 1:

                @pl.when(piece == SEND_AT)
                def _():
                    meet()

                @pl.when(piece >= SEND_AT)
                def _():
                    send1(before)

            if block == 2:

                @pl.when(piece >= MID_AT)
                def _():
                    send2(early)

        return carry

    lax.fori_loop(0, PIECES, one_piece, 0)
    final = PIECES - 1
    filter_x(final, BLOCKS - 1)
    for block in range(BLOCKS):
        transpose(final, block)
    send1(final)

    def rearrange(piece):
        all1(piece).wait_recv()
        run(*[middle(piece, block) for block in range(BLOCKS)])
        send2(piece)

    rearrange(3)
    last(0)
    rearrange(4)
    last(1)
    start(1)
    rearrange(5)
    last(2)
    last(3)
    start(0)
    last(4)
    last(5)

    for side in (0, 1):

        @pl.when(has_prev if side == 0 else has_next)
        def _():
            y_copy(side).wait_recv()

    third = F32(1 / 3)
    scale0 = jnp.where(has_prev, third, F32(1 / 2))
    scale2 = jnp.where(has_next, third, F32(1 / 2))
    for q, p in enumerate(PRODUCTS):
        m0, m2, m1 = whole[0, q], whole[1, q], whole[2, q]
        o_ref[p, 0] = (m0 + m1 + beside[0, q]) * scale0
        o_ref[p, 1] = (m0 + m1 + m2) * third
        o_ref[p, 2] = (m1 + m2 + beside[1, q]) * scale2

    for piece in range(PIECES):
        all1(piece).wait_send()
        all2(piece).wait_send()
    for side in (0, 1):

        @pl.when(has_next if side == 0 else has_prev)
        def _():
            y_copy(side).wait_send()


def solution(mesh):
    placed = P(None, "gy", ("xp", "zp"), None)
    sizes = tuple(mesh.shape[name] for name in ("xp", "zp", "gy"))
    call = pl.pallas_call(
        functools.partial(kernel, sizes),
        out_shape=jax.ShapeDtypeStruct((10, PLANES, 8, 512), F32),
        in_specs=[pl.BlockSpec(memory_space=pl.ANY)] * 2,
        out_specs=pl.BlockSpec(memory_space=pltpu.VMEM),
        scratch_shapes=[
            pltpu.VMEM((PLANES * BLOCKS, 8, 4, ROWS, 128), F32),
            pltpu.VMEM((1280, 256), BF16),
            pltpu.VMEM((2, 8, 2, 4, 16, 128), BF16),
            pltpu.VMEM((BLOCKS, 64, 128), F32),
            pltpu.VMEM((BLOCKS, 64, 128), F32),
            pltpu.VMEM((PIECES + 1, 8, BLOCKS, 8, 128), F32),
            pltpu.VMEM((PIECES + 1, 8, BLOCKS, 8, 128), F32),
            pltpu.VMEM((PIECES + 1, 8, 3, 8, 128), F32),
            pltpu.VMEM((PIECES, 8, 3, 8, 128), F32),
            pltpu.VMEM((PLANES, 10, 8, 512), F32),
            pltpu.VMEM((2, 10, 8, 512), F32),
            pltpu.SemaphoreType.DMA((PLANES * BLOCKS, 8)),
            pltpu.SemaphoreType.DMA,
            pltpu.SemaphoreType.DMA((PIECES,)),
            pltpu.SemaphoreType.DMA((PIECES,)),
            pltpu.SemaphoreType.DMA((PIECES,)),
            pltpu.SemaphoreType.DMA((PIECES,)),
            pltpu.SemaphoreType.DMA((2,)),
            pltpu.SemaphoreType.DMA((2,)),
        ],
        compiler_params=pltpu.CompilerParams(
            collective_id=0, has_side_effects=True, vmem_limit_bytes=60 * 2**20
        ),
    )
    weights = x_weights()

    def per_device(fields):
        return call(fields, jnp.asarray(weights))

    return jax.shard_map(
        per_device, mesh=mesh, in_specs=(placed,), out_specs=placed, check_vma=False
    )
```

profile of v0, /device:TPU:1, one launch (start us, length us, event | category | flops | bytes accessed | tf_op | source)
XLA Modules:
  0.0 39.5 jit_solution(16814157768671494530)
XLA Ops:
  0.0 37.6 %shard_map.28 = f32[10,3,8,512]{3,2,1,0:T(8,128)} custom-call(f32[4,3,64,4096]{3,2,1,0:T(8,128)} %f_hbm.1, bf16[1280,256]{1,0:T(8,128)(2,1)} %constant.2.clone.w_hbm), custom_call_target="tpu_custom_call" | custom-call | tf_op jit(solution)/shard_map/pallas_call | solution.py:464
  37.7 1.8 %copy.4 = f32[10,3,8,512]{3,2,1,0:T(8,128)} copy(f32[10,3,8,512]{3,2,1,0:T(8,128)} %shard_map.28) | data formatting | bytes 983040
where the time goes:
time: 39.6 us; the launch traced here: 39.5 us
  Pallas kernels  37.6 us (95%)
  local copies, waits for them, and re-layouts  1.84 us (5%)
    pallas_call x1, Pallas kernels, per_device(): return call(fields, jnp.asarray(weights))  37.6 us
    unnamed x1, local copies, waits for them, and re-layouts  1.84 us

commit v1 on v0

--- a/solution.py
+++ b/solution.py
@@ -15,7 +15,8 @@
 PLANES, ROWS, NX = 3, 64, 4096
 BLOCKS = 4
 PIECES = 2 * PLANES
-SEND_AT, MID_AT = 1, 3
+STEPS = PIECES * BLOCKS
+SEND_AT, MID_AT, LAST_AT = 4, 14, 27
 
 
 def gauss():
@@ -87,6 +88,10 @@
     return out
 
 
+def far_first(n):
+    return sorted(range(1, n), key=lambda k: -min(k, n - k))
+
+
 def turn(x, shift):
     shift %= 128
     return pltpu.roll(x, shift, 1) if shift else x
@@ -100,26 +105,19 @@
     xp, zp, gy = lax.axis_index("xp"), lax.axis_index("zp"), lax.axis_index("gy")
     has_prev, has_next = gy > 0, gy < n_gy - 1
 
-    def tile_copy(unit, h):
-        tile = lax.rem(unit, BLOCKS) * 8 + h
-        lanes = pl.ds(pl.multiple_of(tile * 128, 128), 128)
+    def fetch(unit):
+        x_tiles = pl.ds(pl.multiple_of(lax.rem(unit, BLOCKS) * 8, 8), 8)
         plane = lax.rem(2 * (unit // BLOCKS), 3)
         return pltpu.make_async_copy(
-            f_hbm.at[:, plane, :, lanes], fields.at[unit, h], f_sem.at[unit, h]
-        )
-
-    def fetch(unit):
-        def one(h, carry):
-            tile_copy(unit, h).start()
-            return carry
-
-        lax.fori_loop(0, 8, one, 0)
+            f_hbm.at[:, plane, :, x_tiles],
+            fields.at[unit].reshape(4, 8, 9, 8, 128).at[:, :, pl.ds(0, 8)],
+            f_sem.at[unit],
+        )
 
     weights = pltpu.make_async_copy(w_hbm, w_ref, w_sem)
     weights.start()
-    fetch(0)
-    for unit in range(1, BLOCKS):
-        fetch(unit)
+    for unit in range(BLOCKS):
+        fetch(unit).start()
 
     barrier = pltpu.get_barrier_semaphore()
 
@@ -154,18 +152,15 @@
     row = lax.broadcasted_iota(jnp.int32, (8, 128), 0)
     lane = lax.broadcasted_iota(jnp.int32, (8, 128), 1)
     lane64 = lax.broadcasted_iota(jnp.int32, (64, 128), 1)
-    main_x[...] = jnp.zeros(main_x.shape, F32)
-    leak_x[...] = jnp.zeros(leak_x.shape, F32)
-    got1[PIECES] = jnp.zeros(got1.shape[1:], F32)
-
-    def filter_z(piece, block, h):
-        slot = block % 2
+    def filter_z(step, h):
+        piece, block = step // BLOCKS, lax.rem(step, BLOCKS)
+        slot = lax.rem(step, 2)
         unit = (piece // 2) * BLOCKS + block
         half = lax.rem(piece, 2)
         names = (2 * half, 1 + 2 * half, 2 - half, 3 - 3 * half)
 
         def load(f, b):
-            return fields[unit, h, names[f], pl.ds(b, 8, stride=8), :]
+            return fields[unit, pl.ds(names[f] * 576 + h * 8 + b, 8, stride=72), :]
 
         rows = z_stage(load, row)
         four_ends = (row < 2) | (row > 5)
@@ -179,8 +174,9 @@
             held[slot, h, 0, k] = high
             held[slot, h, 1, k] = (both - high.astype(F32)).astype(BF16)
 
-    def filter_x(piece, block):
-        cells = [held[block % 2, h].reshape(128, 128) for h in range(8)]
+    def filter_x(step):
+        block, slot = lax.rem(step, BLOCKS), lax.rem(step, 2)
+        cells = [held[slot, h].reshape(128, 128) for h in range(8)]
 
         def product(values, weight):
             r = jnp.dot(values, weight, preferred_element_type=F32)
@@ -189,11 +185,14 @@
         main_x[block] = product(jnp.concatenate(cells, axis=1), w_ref[0:1024])
         leak_x[block] = product(jnp.concatenate([cells[0], cells[7]], axis=1), w_ref[1024:1280])
 
-    def transpose(piece, block):
-        before, after = leak_x[(block + 3) % BLOCKS], leak_x[(block + 1) % BLOCKS]
-        x = main_x[block] + jnp.where(lane64 < 2, before, jnp.where(lane64 > 125, after, 0.0))
-        y = jnp.transpose(jnp.concatenate([x, pltpu.roll(x, 64, 1)], axis=0))
-        sent1[piece, :, block] = y[:64].reshape(8, 8, 128)
+    def transpose(piece, pair):
+        both = []
+        for block in (2 * pair, 2 * pair + 1):
+            before, after = leak_x[(block + 3) % BLOCKS], leak_x[(block + 1) % BLOCKS]
+            both.append(main_x[block] + jnp.where(lane64 < 2, before, jnp.where(lane64 > 125, after, 0.0)))
+        y = jnp.transpose(jnp.concatenate(both, axis=0))
+        for k in range(2):
+            sent1[piece, :, 2 * pair + k] = y[64 * k : 64 * k + 64].reshape(8, 8, 128)
 
     def copy1(piece, to):
         return pltpu.make_async_remote_copy(
@@ -251,12 +250,12 @@
             y_copy(side).start()
 
     def send1(piece):
-        for k in range(1, n_zp):
+        for k in far_first(n_zp):
             copy1(piece, lax.rem(zp + k, n_zp)).start()
         got1[piece, zp] = sent1[piece, zp]
 
     def send2(piece):
-        for k in range(1, n_xp):
+        for k in far_first(n_xp):
             copy2(piece, lax.rem(xp + k, n_xp)).start()
         got2[piece, xp] = sent2[piece, xp]
 
@@ -283,137 +282,113 @@
             z = turn(jnp.where(outer, z, 0.0), 4 * j + 2)
             out = z if out is None else out + z
         yield
-        w = [turn(x, 64) for x in v[:5]]
-        flip = turn(out, 64)
-        rest = (jnp.where(first_two, flip, out), jnp.where(first_two, out, flip))
-        for k in range(2):
-            low = v if k == 0 else w
-            high = w if k == 0 else v
-            to = 2 * block + k
-            sent2[piece, to, 0] = jnp.where(left, low[0], high[1])
-            sent2[piece, to, 1] = jnp.where(left, low[2], high[3])
-            sent2[piece, to, 2] = jnp.where(left, low[4], rest[k])
+        to = 4 * (block // 2) + block % 2
+        for k in range(3):
+            x, y = v[2 * k], v[2 * k + 1] if k < 2 else out
+            swap = turn(jnp.where(left, y, x), 64)
+            if k < 2:
+                low, high = swap, y
+            else:
+                low, high = jnp.where(first_two, swap, y), jnp.where(first_two, y, swap)
+            sent2[piece, to, k] = jnp.where(left, x, low)
+            sent2[piece, to + 2, k] = jnp.where(left, swap, high)
 
     def last(piece):
         all2(piece).wait_recv()
         plane, half = piece // 2, lax.rem(piece, 2)
         e = [got2[piece, d, 2] for d in range(8)]
+        around = []
+        for g in range(4):
+            near = jnp.where(first_two, e[2 * g + 1], e[2 * g])
+            far = jnp.where(first_two, e[(2 * g + 2) % 8], e[(2 * g + 7) % 8])
+            around.append(jnp.where(left, turn(far, 64), near))
         for j in range(5):
-            m = [got2[piece, d, j // 2] for d in range(8)]
-            near = [turn(x, -2 - 4 * j) for x in e]
-            far = [turn(x, 62 - 4 * j) for x in e]
             for g in range(4):
-                a, b = m[2 * g], m[2 * g + 1]
-                if j % 2 == 0:
-                    main = jnp.where(left, a, turn(b, 64))
-                else:
-                    main = jnp.where(left, turn(a, 64), b)
-                z = jnp.where(lane < 2, far[(2 * g + 7) % 8], far[(2 * g + 2) % 8])
-                z = jnp.where((lane > 61) & (lane < 64), near[2 * g + 1], z)
-                z = jnp.where((lane > 63) & (lane < 66), near[2 * g], z)
+                a, b = got2[piece, 2 * g, j // 2], got2[piece, 2 * g + 1, j // 2]
+                main = jnp.where(left, a, turn(b, 64)) if j % 2 == 0 else jnp.where(left, turn(a, 64), b)
+                z = turn(around[g], -2 - 4 * j)
                 whole[plane, half * 5 + j, :, pl.ds(g * 128, 128)] = main + jnp.where(outer, z, 0.0)
-
-    def run(*parts):
-        parts = list(parts)
-        while parts:
-            parts = [part for part in parts if next(part, parts) is not parts]
-
-    def one_piece(piece, carry):
-        before = jnp.where(piece >= SEND_AT, piece - SEND_AT, PIECES)
-        early = jnp.where(piece >= MID_AT, piece - MID_AT, PIECES)
-        for block in range(BLOCKS):
-
-            @pl.when(lax.rem(piece, 2) == 0)
-            def _():
-                for h in range(8):
-                    tile_copy((piece // 2) * BLOCKS + block, h).wait()
-
-            if block == 0:
-
-                @pl.when(piece == 0)
-                def _():
-                    weights.wait()
-
-                @pl.when(lax.rem(piece, 2) == 0)
-                def _():
-                    @pl.when(piece // 2 < PLANES - 1)
-                    def _():
-                        for later in range(BLOCKS):
-                            fetch((piece // 2 + 1) * BLOCKS + later)
-
-            if block == 2:
-
-                @pl.when(piece >= MID_AT)
-                def _():
-                    all1(early).wait_recv()
-
-            work = []
-            if block == 1:
-                for part in range(BLOCKS):
-                    transpose(before, part)
-            if block == 2:
-                work = [middle(early, part) for part in range(BLOCKS)]
-            filter_x(piece, (block + 3) % BLOCKS)
-            for h in range(8):
-                work = [part for part in work if next(part, work) is not work]
-                filter_z(piece, block, h)
-            run(*work)
-            if block == 1:
-
-                @pl.when(piece == SEND_AT)
-                def _():
-                    meet()
-
-                @pl.when(piece >= SEND_AT)
-                def _():
-                    send1(before)
-
-            if block == 2:
-
-                @pl.when(piece >= MID_AT)
-                def _():
-                    send2(early)
-
-        return carry
-
-    lax.fori_loop(0, PIECES, one_piece, 0)
-    final = PIECES - 1
-    filter_x(final, BLOCKS - 1)
-    for block in range(BLOCKS):
-        transpose(final, block)
-    send1(final)
-
-    def rearrange(piece):
-        all1(piece).wait_recv()
-        run(*[middle(piece, block) for block in range(BLOCKS)])
-        send2(piece)
-
-    rearrange(3)
-    last(0)
-    rearrange(4)
-    last(1)
-    start(1)
-    rearrange(5)
-    last(2)
-    last(3)
-    start(0)
-    last(4)
-    last(5)
-
-    for side in (0, 1):
-
-        @pl.when(has_prev if side == 0 else has_next)
-        def _():
-            y_copy(side).wait_recv()
 
     third = F32(1 / 3)
     scale0 = jnp.where(has_prev, third, F32(1 / 2))
     scale2 = jnp.where(has_next, third, F32(1 / 2))
-    for q, p in enumerate(PRODUCTS):
-        m0, m2, m1 = whole[0, q], whole[1, q], whole[2, q]
-        o_ref[p, 0] = (m0 + m1 + beside[0, q]) * scale0
-        o_ref[p, 1] = (m0 + m1 + m2) * third
-        o_ref[p, 2] = (m1 + m2 + beside[1, q]) * scale2
+
+    def box(half):
+        for q in range(5 * half, 5 * half + 5):
+            p, m0, m2, m1 = PRODUCTS[q], whole[0, q], whole[1, q], whole[2, q]
+            o_ref[p, 0] = (m0 + m1 + beside[0, q]) * scale0
+            o_ref[p, 1] = (m0 + m1 + m2) * third
+            o_ref[p, 2] = (m1 + m2 + beside[1, q]) * scale2
+
+    def one_step(step, carry):
+        block = lax.rem(step, BLOCKS)
+
+        @pl.when((step < STEPS) & (lax.rem(step, 2 * BLOCKS) < BLOCKS))
+        def _():
+            fetch((step // (2 * BLOCKS)) * BLOCKS + block).wait()
+
+        @pl.when(step == 0)
+        def _():
+            weights.wait()
+
+        @pl.when(step < STEPS)
+        def _():
+            filter_x(step + STEPS - 1)
+            for h in range(8):
+                filter_z(step, h)
+
+        @pl.when(step == STEPS)
+        def _():
+            filter_x(step - 1)
+
+        @pl.when(step == SEND_AT)
+        def _():
+            meet()
+
+        @pl.when((block == SEND_AT % BLOCKS) & (step >= SEND_AT) & (step <= STEPS))
+        def _():
+            piece = (step - SEND_AT) // BLOCKS
+            transpose(piece, 0)
+            transpose(piece, 1)
+            send1(piece)
+
+        @pl.when((step >= 1) & (step <= (PLANES - 1) * BLOCKS))
+        def _():
+            fetch(step + BLOCKS - 1).start()
+
+        @pl.when((block == MID_AT % BLOCKS) & (step >= MID_AT) & (step < MID_AT + PIECES * BLOCKS))
+        def _():
+            piece = (step - MID_AT) // BLOCKS
+            all1(piece).wait_recv()
+            work = [middle(piece, part) for part in range(BLOCKS)]
+            while work:
+                work = [part for part in work if next(part, work) is not work]
+            send2(piece)
+
+        @pl.when((step == LAST_AT) | (step == LAST_AT + BLOCKS) | (step >= LAST_AT + 2 * BLOCKS))
+        def _():
+            last(jnp.where(step > LAST_AT + BLOCKS, step - LAST_AT - 2 * BLOCKS + 2, (step - LAST_AT) // BLOCKS))
+
+        @pl.when(step == LAST_AT + BLOCKS)
+        def _():
+            start(1)
+
+        @pl.when(step == LAST_AT + 2 * BLOCKS + 1)
+        def _():
+            start(0)
+
+        return carry
+
+    lax.fori_loop(0, LAST_AT + 2 * BLOCKS + 3, one_step, 0)
+    for side in (0, 1):
+
+        @pl.when(has_prev if side == 0 else has_next)
+        def _():
+            y_copy(side).wait_recv()
+
+    box(0)
+    last(PIECES - 1)
+    box(1)
 
     for piece in range(PIECES):
         all1(piece).wait_send()
@@ -430,22 +405,22 @@
     sizes = tuple(mesh.shape[name] for name in ("xp", "zp", "gy"))
     call = pl.pallas_call(
         functools.partial(kernel, sizes),
-        out_shape=jax.ShapeDtypeStruct((10, PLANES, 8, 512), F32),
+        out_shape=pltpu.VMEM((10, PLANES, 8, 512), F32),
         in_specs=[pl.BlockSpec(memory_space=pl.ANY)] * 2,
         out_specs=pl.BlockSpec(memory_space=pltpu.VMEM),
         scratch_shapes=[
-            pltpu.VMEM((PLANES * BLOCKS, 8, 4, ROWS, 128), F32),
+            pltpu.VMEM((PLANES * BLOCKS, 4 * ROWS * 9, 128), F32),
             pltpu.VMEM((1280, 256), BF16),
             pltpu.VMEM((2, 8, 2, 4, 16, 128), BF16),
             pltpu.VMEM((BLOCKS, 64, 128), F32),
             pltpu.VMEM((BLOCKS, 64, 128), F32),
-            pltpu.VMEM((PIECES + 1, 8, BLOCKS, 8, 128), F32),
-            pltpu.VMEM((PIECES + 1, 8, BLOCKS, 8, 128), F32),
-            pltpu.VMEM((PIECES + 1, 8, 3, 8, 128), F32),
+            pltpu.VMEM((PIECES, 8, BLOCKS, 8, 128), F32),
+            pltpu.VMEM((PIECES, 8, BLOCKS, 8, 128), F32),
+            pltpu.VMEM((PIECES, 8, 3, 8, 128), F32),
             pltpu.VMEM((PIECES, 8, 3, 8, 128), F32),
             pltpu.VMEM((PLANES, 10, 8, 512), F32),
             pltpu.VMEM((2, 10, 8, 512), F32),
-            pltpu.SemaphoreType.DMA((PLANES * BLOCKS, 8)),
+            pltpu.SemaphoreType.DMA((PLANES * BLOCKS,)),
             pltpu.SemaphoreType.DMA,
             pltpu.SemaphoreType.DMA((PIECES,)),
             pltpu.SemaphoreType.DMA((PIECES,)),
@@ -461,7 +436,8 @@
     weights = x_weights()
 
     def per_device(fields):
-        return call(fields, jnp.asarray(weights))
+        tiles = fields.reshape(4, PLANES, ROWS // 8, 8, NX // 128, 128).transpose(0, 1, 2, 4, 3, 5)
+        return call(tiles, jnp.asarray(weights))
 
     return jax.shard_map(
         per_device, mesh=mesh, in_specs=(placed,), out_specs=placed, check_vma=False

time: 39.6 us -> 33 us (0.83)
  Pallas kernels: 37.6 us -> 32.1 us
  local copies, waits for them, and re-layouts: 1.84 us -> 0.78 us
    pallas_call x1, Pallas kernels: 37.6 us -> 32.1 us  [per_device(): return call(tiles, jnp.asarray(weights))]
    unnamed x1, local copies, waits for them, and re-layouts: 1.84 us -> 0.78 us
where the time goes in v1:
time: 33 us; the launch traced here: 32.9 us
  Pallas kernels  32.1 us (97%)
  local copies, waits for them, and re-layouts  0.78 us (2%)
    pallas_call x1, Pallas kernels, per_device(): return call(tiles, jnp.asarray(weights))  32.1 us
    unnamed x1, local copies, waits for them, and re-layouts  0.78 us

profile of v1, /device:TPU:1, one launch (start us, length us, event | category | flops | bytes accessed | tf_op | source)
XLA Modules:
  0.0 32.9 jit_solution(2689055652893269145)
XLA Ops:
  0.0 32.1 %shard_map.28 = f32[10,3,8,512]{3,2,1,0:T(8,128)S(1)} custom-call(f32[4,3,8,32,8,128]{5,4,3,2,1,0:T(8,128)} %bitcast.3, bf16[1280,256]{1,0:T(8,128)(2,1)} %constant.2.clone.w_hbm), custom_call_target="tpu_custom_call" | custom-call | tf_op jit(solution)/shard_map/pallas_call | solution.py:440
  32.1 0.8 %copy.4 = f32[10,3,8,512]{3,2,1,0:T(8,128)} copy(f32[10,3,8,512]{3,2,1,0:T(8,128)S(1)} %shard_map.28) | data formatting | bytes 983040

commit v2 on v1

--- a/solution.py
+++ b/solution.py
@@ -116,7 +116,7 @@
 
     weights = pltpu.make_async_copy(w_hbm, w_ref, w_sem)
     weights.start()
-    for unit in range(BLOCKS):
+    for unit in range(PLANES * BLOCKS):
         fetch(unit).start()
 
     barrier = pltpu.get_barrier_semaphore()
@@ -265,20 +265,19 @@
     first_two = lax.rem(lane, 4) < 2
 
     def middle(piece, block):
-        v = [got1[piece, k, block] for k in range(8)]
-        for s in (4, 2, 1):
+        v = [turn(got1[piece, k, block], 8 * k) for k in range(8)]
+        yield
+        for s in (1, 2, 4):
             bit = (group & s) == 0
-            for a in range(8):
-                if a & s == 0:
-                    x, y = v[a], v[a + s]
-                    v[a] = jnp.where(bit, x, turn(y, 8 * s))
-                    v[a + s] = jnp.where(bit, turn(x, -8 * s), y)
-            yield
+            v = [jnp.where(bit, v[k], v[(k + s) % 8]) for k in range(8)]
+        yield
+        v = [v[-j % 8] for j in range(8)]
         out = None
         for j in range(5):
-            e, shift = v[5 + j // 2], 8 if j % 2 == 0 else 4
-            z = jnp.where(within < 2, turn(e, shift), jnp.where(within > 5, turn(e, -shift), 0.0))
-            v[j] = v[j] + jnp.where(outer, 0.0, z)
+            e, back, shift = v[5 + j // 2], -8 * (5 + j // 2), 8 if j % 2 == 0 else 4
+            up, down = turn(e, back + shift), turn(e, back - shift)
+            z = jnp.where(within < 2, up, jnp.where(within > 5, down, 0.0))
+            v[j] = turn(v[j], -8 * j) + jnp.where(outer, 0.0, z)
             z = turn(jnp.where(outer, z, 0.0), 4 * j + 2)
             out = z if out is None else out + z
         yield
@@ -351,10 +350,6 @@
             transpose(piece, 0)
             transpose(piece, 1)
             send1(piece)
-
-        @pl.when((step >= 1) & (step <= (PLANES - 1) * BLOCKS))
-        def _():
-            fetch(step + BLOCKS - 1).start()
 
         @pl.when((block == MID_AT % BLOCKS) & (step >= MID_AT) & (step < MID_AT + PIECES * BLOCKS))
         def _():

time: 33 us -> 32.3 us (0.979)
  Pallas kernels: 32.1 us -> 31.3 us
    pallas_call x1, Pallas kernels: 32.1 us -> 31.3 us  [per_device(): return call(tiles, jnp.asarray(weights))]
where the time goes in v2:
time: 32.3 us; the launch traced here: 32.1 us
  Pallas kernels  31.3 us (97%)
  local copies, waits for them, and re-layouts  0.78 us (2%)
    pallas_call x1, Pallas kernels, per_device(): return call(tiles, jnp.asarray(weights))  31.3 us
    unnamed x1, local copies, waits for them, and re-layouts  0.78 us

profile of v2, /device:TPU:1, one launch (start us, length us, event | category | flops | bytes accessed | tf_op | source)
XLA Modules:
  0.0 32.1 jit_solution(18385608028684357243)
XLA Ops:
  0.0 31.3 %shard_map.28 = f32[10,3,8,512]{3,2,1,0:T(8,128)S(1)} custom-call(f32[4,3,8,32,8,128]{5,4,3,2,1,0:T(8,128)} %bitcast.3, bf16[1280,256]{1,0:T(8,128)(2,1)} %constant.2.clone.w_hbm), custom_call_target="tpu_custom_call" | custom-call | tf_op jit(solution)/shard_map/pallas_call | solution.py:435
  31.3 0.8 %copy.4 = f32[10,3,8,512]{3,2,1,0:T(8,128)} copy(f32[10,3,8,512]{3,2,1,0:T(8,128)S(1)} %shard_map.28) | data formatting | bytes 983040

commit v3 on v2

--- a/solution.py
+++ b/solution.py
@@ -254,10 +254,14 @@
             copy1(piece, lax.rem(zp + k, n_zp)).start()
         got1[piece, zp] = sent1[piece, zp]
 
-    def send2(piece):
-        for k in far_first(n_xp):
-            copy2(piece, lax.rem(xp + k, n_xp)).start()
-        got2[piece, xp] = sent2[piece, xp]
+    def send2(piece, to):
+        @pl.when(xp != to)
+        def _():
+            copy2(piece, to).start()
+
+        @pl.when(xp == to)
+        def _():
+            got2[piece, to] = sent2[piece, to]
 
     group, within = lane // 8, lax.rem(lane, 8)
     outer = (lane < 2) | (lane > 125) | ((lane > 61) & (lane < 66))
@@ -355,10 +359,12 @@
         def _():
             piece = (step - MID_AT) // BLOCKS
             all1(piece).wait_recv()
-            work = [middle(piece, part) for part in range(BLOCKS)]
-            while work:
-                work = [part for part in work if next(part, work) is not work]
-            send2(piece)
+            for pair in (0, 2):
+                work = [middle(piece, pair), middle(piece, pair + 1)]
+                while work:
+                    work = [part for part in work if next(part, work) is not work]
+                for to in range(2 * pair, 2 * pair + 4):
+                    send2(piece, to)
 
         @pl.when((step == LAST_AT) | (step == LAST_AT + BLOCKS) | (step >= LAST_AT + 2 * BLOCKS))
         def _():
@@ -375,6 +381,7 @@
         return carry
 
     lax.fori_loop(0, LAST_AT + 2 * BLOCKS + 3, one_step, 0)
+    last(PIECES - 1)
     for side in (0, 1):
 
         @pl.when(has_prev if side == 0 else has_next)
@@ -382,7 +389,6 @@
             y_copy(side).wait_recv()
 
     box(0)
-    last(PIECES - 1)
     box(1)
 
     for piece in range(PIECES):

time: 32.3 us -> 32.9 us (1.019)
  Pallas kernels: 31.3 us -> 32 us
    pallas_call x1, Pallas kernels: 31.3 us -> 32 us  [per_device(): return call(tiles, jnp.asarray(weights))]
where the time goes in v3:
time: 32.9 us; the launch traced here: 32.8 us
  Pallas kernels  32 us (97%)
  local copies, waits for them, and re-layouts  0.78 us (2%)
    pallas_call x1, Pallas kernels, per_device(): return call(tiles, jnp.asarray(weights))  32 us
    unnamed x1, local copies, waits for them, and re-layouts  0.78 us

profile of v3, /device:TPU:1, one launch (start us, length us, event | category | flops | bytes accessed | tf_op | source)
XLA Modules:
  0.0 32.8 jit_solution(7662606390987716998)
XLA Ops:
  0.0 32.0 %shard_map.28 = f32[10,3,8,512]{3,2,1,0:T(8,128)S(1)} custom-call(f32[4,3,8,32,8,128]{5,4,3,2,1,0:T(8,128)} %bitcast.3, bf16[1280,256]{1,0:T(8,128)(2,1)} %constant.2.clone.w_hbm), custom_call_target="tpu_custom_call" | custom-call | tf_op jit(solution)/shard_map/pallas_call | solution.py:441
  32.0 0.8 %copy.4 = f32[10,3,8,512]{3,2,1,0:T(8,128)} copy(f32[10,3,8,512]{3,2,1,0:T(8,128)S(1)} %shard_map.28) | data formatting | bytes 983040

commit v4 on v2

--- a/solution.py
+++ b/solution.py
@@ -375,6 +375,7 @@
         return carry
 
     lax.fori_loop(0, LAST_AT + 2 * BLOCKS + 3, one_step, 0)
+    last(PIECES - 1)
     for side in (0, 1):
 
         @pl.when(has_prev if side == 0 else has_next)
@@ -382,7 +383,6 @@
             y_copy(side).wait_recv()
 
     box(0)
-    last(PIECES - 1)
     box(1)
 
     for piece in range(PIECES):

time: 32.3 us -> 32.3 us (level)
  no operation moved by 1% of the time
where the time goes in v4:
time: 32.3 us; the launch traced here: 32.1 us
  Pallas kernels  31.3 us (97%)
  local copies, waits for them, and re-layouts  0.78 us (2%)
    pallas_call x1, Pallas kernels, per_device(): return call(tiles, jnp.asarray(weights))  31.3 us
    unnamed x1, local copies, waits for them, and re-layouts  0.78 us

profile of v4, /device:TPU:1, one launch (start us, length us, event | category | flops | bytes accessed | tf_op | source)
XLA Modules:
  0.0 32.1 jit_solution(8138856458791507389)
XLA Ops:
  0.0 31.3 %shard_map.28 = f32[10,3,8,512]{3,2,1,0:T(8,128)S(1)} custom-call(f32[4,3,8,32,8,128]{5,4,3,2,1,0:T(8,128)} %bitcast.3, bf16[1280,256]{1,0:T(8,128)(2,1)} %constant.2.clone.w_hbm), custom_call_target="tpu_custom_call" | custom-call | tf_op jit(solution)/shard_map/pallas_call | solution.py:435
  31.3 0.8 %copy.4 = f32[10,3,8,512]{3,2,1,0:T(8,128)} copy(f32[10,3,8,512]{3,2,1,0:T(8,128)S(1)} %shard_map.28) | data formatting | bytes 983040
